TPU v7x, 32 devices: a whole 2x2x4 slice. The times are simulated.
32 devices in a mesh: grp: 1, dap: 16 (over z, y, x), ch: 1, sub: 2 (over core).
Axes of the slice: x: 2, y: 2, z: 4, core: 2. Of those that a mesh axis runs over, the one named last changes fastest.
Arguments:
- query_act: bfloat16 [4, 32, 256, 384], P('ch', None, ('grp', 'dap', 'sub')), may hold values from -8 to 8
- key_act: bfloat16 [4, 32, 256, 384], P('ch', None, ('grp', 'dap', 'sub')), may hold values from -6 to 6
- value_act: bfloat16 [4, 32, 256, 384], P('ch', None, ('grp', 'dap', 'sub')), may hold values from -6 to 6
- gate_act: bfloat16 [4, 32, 256, 384], P('ch', None, ('grp', 'dap', 'sub')), may hold values from -6 to 6
- grad_out: bfloat16 [4, 32, 256, 384], P('ch', None, ('grp', 'dap', 'sub')), may hold values from -6 to 6
- bias_pair: bfloat16 [4, 384, 384], P('ch', ('grp', 'dap', 'sub')), may hold values from -6 to 6
- residue_mask: int32 [384], P('grp'), may hold values 0 or 1
- chain_index: int32 [384], P('grp'), may hold values from 0 to 5, never falling along the last dimension, each value on 1 to 128 neighbouring positions
- chain_bias: float32 [4], P('ch'), may hold values from -2 to 2
Outputs:
- grad_query: bfloat16 [4, 32, 256, 384], P('ch', None, ('grp', 'dap', 'sub'))
- grad_key: bfloat16 [4, 32, 256, 384], P('ch', None, ('grp', 'dap', 'sub'))
- grad_value: bfloat16 [4, 32, 256, 384], P('ch', None, ('grp', 'dap', 'sub'))
- grad_gate: bfloat16 [4, 32, 256, 384], P('ch', None, ('grp', 'dap', 'sub'))
- grad_bias: float32 [4, 384, 384], P('ch', ('grp', 'dap', 'sub'))
All inputs are finite; a program needn't handle non-finite values.
Results may differ from a plain program's by a relative error of at most 0.025.
Values may be sent and summed in bfloat16 or wider, within the bound.
A program may use at most 64 MiB of HBM per device.

v0:
```python
import jax
import jax.numpy as jnp
from jax import lax
from jax.sharding import PartitionSpec as P


def pair_bias(gathered, residue_mask, chain_index, chain_bias):
    same_chain = (chain_index[:, None] == chain_index[None, :]).astype(jnp.float32)
    key_block = jnp.where(residue_mask > 0, 0.0, -1000000000.0).astype(jnp.float32)
    return (
        gathered.astype(jnp.float32)
        + chain_bias[:, None, None] * same_chain[None]
        + key_block[None, None, :]
    )


def row_grads(full_bias, query_row, key_row, value_row, gate_row, cotangent):
    score_scale = query_row.shape[1] ** (-0.5)
    scores = (
        jnp.einsum("hdj,hdk->hjk", query_row, key_row, preferred_element_type=jnp.float32)
        * score_scale
        + full_bias
    )
    attn_probs = jax.nn.softmax(scores, axis=-1)
    probs_low = attn_probs.astype(jnp.bfloat16)
    attended = jnp.einsum("hjk,hdk->hdj", probs_low, value_row, preferred_element_type=jnp.float32)
    sigmoid_gate = jax.nn.sigmoid(gate_row.astype(jnp.float32))
    cotangent_wide = cotangent.astype(jnp.float32)
    grad_gate = (cotangent_wide * attended * sigmoid_gate * (1.0 - sigmoid_gate)).astype(
        jnp.bfloat16
    )
    grad_att = (cotangent_wide * sigmoid_gate).astype(jnp.bfloat16)
    grad_value = jnp.einsum(
        "hjk,hdj->hdk", probs_low, grad_att, preferred_element_type=jnp.float32
    ).astype(jnp.bfloat16)
    grad_probs = jnp.einsum("hdj,hdk->hjk", grad_att, value_row, preferred_element_type=jnp.float32)
    row_delta = jnp.sum(grad_att.astype(jnp.float32) * attended, axis=1)
    grad_scores = attn_probs * (grad_probs - row_delta[:, :, None])
    scores_low = grad_scores.astype(jnp.bfloat16)
    grad_query = (
        score_scale
        * jnp.einsum("hjk,hdk->hdj", scores_low, key_row, preferred_element_type=jnp.float32)
    ).astype(jnp.bfloat16)
    grad_key = (
        score_scale
        * jnp.einsum("hjk,hdj->hdk", scores_low, query_row, preferred_element_type=jnp.float32)
    ).astype(jnp.bfloat16)
    return (grad_scores, (grad_query, grad_key, grad_value, grad_gate))


def per_device(
    query_act,
    key_act,
    value_act,
    gate_act,
    grad_out,
    bias_pair,
    residue_mask,
    chain_index,
    chain_bias,
):
    gathered = lax.all_gather(bias_pair, ("dap", "sub"), axis=1, tiled=True)
    full_bias = pair_bias(gathered, residue_mask, chain_index, chain_bias)

    def row_step(running, row_inputs):
        grad_scores, grads = row_grads(full_bias, *row_inputs)
        return (running + grad_scores, grads)

    stacked = tuple(
        (
            jnp.moveaxis(member, 2, 0)
            for member in (query_act, key_act, value_act, gate_act, grad_out)
        )
    )
    running, grads = lax.scan(row_step, jnp.zeros(full_bias.shape, jnp.float32), stacked)
    grad_query, grad_key, grad_value, grad_gate = (jnp.moveaxis(member, 0, 2) for member in grads)
    grad_bias = lax.psum_scatter(running, ("dap", "sub"), scatter_dimension=1, tiled=True)
    return (grad_query, grad_key, grad_value, grad_gate, grad_bias)


def solution(mesh):
    placed = (
        P("ch", None, ("grp", "dap", "sub"), None),
        P("ch", None, ("grp", "dap", "sub"), None),
        P("ch", None, ("grp", "dap", "sub"), None),
        P("ch", None, ("grp", "dap", "sub"), None),
        P("ch", None, ("grp", "dap", "sub"), None),
        P("ch", ("grp", "dap", "sub"), None),
        P("grp"),
        P("grp"),
        P("ch"),
    )
    return jax.shard_map(
        per_device,
        mesh=mesh,
        in_specs=placed,
        out_specs=(
            P("ch", None, ("grp", "dap", "sub"), None),
            P("ch", None, ("grp", "dap", "sub"), None),
            P("ch", None, ("grp", "dap", "sub"), None),
            P("ch", None, ("grp", "dap", "sub"), None),
            P("ch", ("grp", "dap", "sub"), None),
        ),
        check_vma=False,
    )
```

profile of v0, /device:TPU:0, one launch (start us, length us, event | category | flops | bytes accessed | tf_op | source)
XLA Modules:
  0.0 321.4 jit_solution(3497017570433674483)
XLA Ops:
  8.0 1.4 copy.64
  10.1 1.7 compare_convert_fusion
  11.8 1.4 copy_bitcast_fusion.6
  13.3 1.5 copy_bitcast_fusion.4
  14.7 53.0 %all-gather.2.cloned.1.call-done = bf16[4,384,384]{2,0,1:T(4,128)(2,1)} async-done(((bf16[4,12,384]{2,0,1:T(4,128)(2,1)}), bf16[4,384,384]{2,0,1:T(4,128)(2,1)}) %all-gather.2.cloned.1.call-update) | async-done | bytes 1179664 | tf_op jit(solution)/shard_map/all_gather | solution.py:62
  67.7 2.1 add_add_fusion
  69.8 2.6 copy.40
  72.4 102.3 %while.19 = (s32[]{:T(128)}, f32[4,384,384]{1,2,0:T(8,128)}, bf16[8,4,32,384]{3,2,1,0:T(8,128)(2,1)}, bf16[8,4,32,384]{3,2,1,0:T(8,128)(2,1)}, bf16[8,4,32,384]{...) while((s32[]{:T(128)}, f32[4,384,384]{1,2,0:T(8,128)}, ...), condition=%wide.region_4.5_spmd.clone, body=%wide.region_0.4_spmd.clone.sunk | while | flops 235486080 | bytes 48599816 | solution.py:75
  72.4 2.6 fusion.81
  79.6 2.4 select_add_fusion.2
  82.0 1.4 fusion.84
  83.4 1.8 fusion.83
  85.2 2.6 fusion.81
  92.4 2.4 select_add_fusion.2
  94.7 1.4 fusion.84
  96.2 1.8 fusion.83
  98.0 2.6 fusion.81
  102.0 1.3 multiply_reduce_fusion.2
  105.2 2.4 select_add_fusion.2
  107.5 1.4 fusion.84
  108.9 1.8 fusion.83
  110.8 2.6 fusion.81
  114.7 1.3 multiply_reduce_fusion.2
  117.9 2.4 select_add_fusion.2
  120.3 1.4 fusion.84
  121.7 1.8 fusion.83
  123.5 2.6 fusion.81
  127.5 1.3 multiply_reduce_fusion.2
  130.7 2.4 select_add_fusion.2
  133.1 1.4 fusion.84
  134.5 1.8 fusion.83
  136.3 2.6 fusion.81
  143.5 2.4 select_add_fusion.2
  145.9 1.4 fusion.84
  147.3 1.8 fusion.83
  149.1 2.6 fusion.81
  153.1 1.3 multiply_reduce_fusion.2
  156.3 2.4 select_add_fusion.2
  158.6 1.4 fusion.84
  160.1 1.8 fusion.83
  161.9 2.6 fusion.81
  165.9 1.3 multiply_reduce_fusion.2
  169.1 2.4 select_add_fusion.2
  171.4 1.4 fusion.84
  172.8 1.8 fusion.83
  174.7 4.3 %copy.45 = f32[4,384,384]{2,0,1:T(4,128)} copy(f32[4,384,384]{1,2,0:T(8,128)} %get-tuple-element.75) | data formatting | bytes 4718592 | tf_op jit(solution)/shard_map/while | solution.py:75
  185.4 127.7 %all-reduce.3.cloned.1.call-done = f32[4,384,384]{2,0,1:T(4,128)} async-done(((f32[4,384,384]{2,0,1:T(4,128)}), f32[4,384,384]{2,0,1:T(4,128)}) %all-reduce.3.cloned.1.call-update) | async-done | bytes 2359312
  313.1 1.5 constant_dynamic-slice_fusion
  (123 shorter events, 37.6 us)
Async XLA Ops:
  7.2 4.6 %copy-start.8 = (bf16[4,32,8,384]{3,2,1,0:T(8,128)(2,1)S(1)}, bf16[4,32,8,384]{3,2,1,0:T(8,128)(2,1)}, u32[]{:S(2)}) copy-start(bf16[4,32,8,384]{3,2,1,0:T(8,128)(2,1)} %param.15) | copy-start | bytes 2359300
  7.2 4.6 %copy-start.9 = (bf16[4,32,8,384]{3,2,1,0:T(8,128)(2,1)S(1)}, bf16[4,32,8,384]{3,2,1,0:T(8,128)(2,1)}, u32[]{:S(2)}) copy-start(bf16[4,32,8,384]{3,2,1,0:T(8,128)(2,1)} %param.12) | copy-start | bytes 2359300
  7.2 60.5 %all-gather.2.cloned.1.call-start = ((), (), s32[]{:S(2)}) async-start(), calls=%async_computation | async-start | bytes 1216512 | tf_op jit(solution)/shard_map/all_gather | solution.py:62
  7.9 305.2 %all-reduce.3.cloned.1.call-start = ((), (), s32[]{:S(2)}) async-start(), calls=%async_computation.1 | async-start | bytes 4718592
  8.0 5.2 %copy-start.10 = (bf16[4,32,8,384]{3,2,1,0:T(8,128)(2,1)S(1)}, bf16[4,32,8,384]{3,2,1,0:T(8,128)(2,1)}, u32[]{:S(2)}) copy-start(bf16[4,32,8,384]{3,2,1,0:T(8,128)(2,1)} %param.13) | copy-start | bytes 2359300
  8.0 5.2 %copy-start.11 = (bf16[4,32,8,384]{3,2,1,0:T(8,128)(2,1)S(1)}, bf16[4,32,8,384]{3,2,1,0:T(8,128)(2,1)}, u32[]{:S(2)}) copy-start(bf16[4,32,8,384]{3,2,1,0:T(8,128)(2,1)} %param.14) | copy-start | bytes 2359300
  11.8 55.9 %copy-start.12 = (f32[4]{0:T(128)S(1)}, f32[4]{0:T(128)}, u32[]{:S(2)}) copy-start(f32[4]{0:T(128)} %param.19) | copy-start | bytes 52
  75.0 1.1 copy-start.2
  75.0 1.4 copy-start.3
  76.4 3.2 copy-start
  82.0 3.2 %copy-start.1 = (f32[4,384,384]{1,2,0:T(8,128)}, f32[4,384,384]{1,2,0:T(8,128)S(1)}, u32[]{:S(2)}) copy-start(f32[4,384,384]{1,2,0:T(8,128)S(1)} %get-tuple-element.277) | copy-start | bytes 7077892 | tf_op jit(solution)/shard_map/while
  87.8 1.1 copy-start.2
  87.8 1.4 copy-start.3
  89.2 3.2 copy-start
  94.7 3.2 %copy-start.1 = (f32[4,384,384]{1,2,0:T(8,128)}, f32[4,384,384]{1,2,0:T(8,128)S(1)}, u32[]{:S(2)}) copy-start(f32[4,384,384]{1,2,0:T(8,128)S(1)} %get-tuple-element.277) | copy-start | bytes 7077892 | tf_op jit(solution)/shard_map/while
  100.6 1.1 copy-start.2
  100.6 1.4 copy-start.3
  101.9 3.2 copy-start
  107.5 3.2 %copy-start.1 = (f32[4,384,384]{1,2,0:T(8,128)}, f32[4,384,384]{1,2,0:T(8,128)S(1)}, u32[]{:S(2)}) copy-start(f32[4,384,384]{1,2,0:T(8,128)S(1)} %get-tuple-element.277) | copy-start | bytes 7077892 | tf_op jit(solution)/shard_map/while
  113.4 1.1 copy-start.2
  113.4 1.4 copy-start.3
  114.7 3.2 copy-start
  120.3 3.2 %copy-start.1 = (f32[4,384,384]{1,2,0:T(8,128)}, f32[4,384,384]{1,2,0:T(8,128)S(1)}, u32[]{:S(2)}) copy-start(f32[4,384,384]{1,2,0:T(8,128)S(1)} %get-tuple-element.277) | copy-start | bytes 7077892 | tf_op jit(solution)/shard_map/while
  126.1 1.1 copy-start.2
  126.1 1.4 copy-start.3
  127.5 3.2 copy-start
  133.1 3.2 %copy-start.1 = (f32[4,384,384]{1,2,0:T(8,128)}, f32[4,384,384]{1,2,0:T(8,128)S(1)}, u32[]{:S(2)}) copy-start(f32[4,384,384]{1,2,0:T(8,128)S(1)} %get-tuple-element.277) | copy-start | bytes 7077892 | tf_op jit(solution)/shard_map/while
  138.9 1.1 copy-start.2
  138.9 1.4 copy-start.3
  140.3 3.2 copy-start
  145.9 3.2 %copy-start.1 = (f32[4,384,384]{1,2,0:T(8,128)}, f32[4,384,384]{1,2,0:T(8,128)S(1)}, u32[]{:S(2)}) copy-start(f32[4,384,384]{1,2,0:T(8,128)S(1)} %get-tuple-element.277) | copy-start | bytes 7077892 | tf_op jit(solution)/shard_map/while
  151.7 1.1 copy-start.2
  151.7 1.4 copy-start.3
  153.1 3.2 copy-start
  158.6 3.2 %copy-start.1 = (f32[4,384,384]{1,2,0:T(8,128)}, f32[4,384,384]{1,2,0:T(8,128)S(1)}, u32[]{:S(2)}) copy-start(f32[4,384,384]{1,2,0:T(8,128)S(1)} %get-tuple-element.277) | copy-start | bytes 7077892 | tf_op jit(solution)/shard_map/while
  164.5 1.1 copy-start.2
  164.5 1.4 copy-start.3
  165.9 3.2 copy-start
  171.4 3.2 %copy-start.1 = (f32[4,384,384]{1,2,0:T(8,128)}, f32[4,384,384]{1,2,0:T(8,128)S(1)}, u32[]{:S(2)}) copy-start(f32[4,384,384]{1,2,0:T(8,128)S(1)} %get-tuple-element.277) | copy-start | bytes 7077892 | tf_op jit(solution)/shard_map/while
  178.9 1.1 copy-start.4
  178.9 2.5 copy-start.7
  178.9 3.8 %copy-start.6 = (bf16[8,4,32,384]{3,2,1,0:T(8,128)(2,1)S(1)}, bf16[8,4,32,384]{3,2,1,0:T(8,128)(2,1)}, u32[]{:S(2)}) copy-start(bf16[8,4,32,384]{3,2,1,0:T(8,128)(2,1)} %get-tuple-element.72) | copy-start | bytes 2359300
  180.1 4.0 %copy-start.5 = (bf16[8,4,32,384]{3,2,1,0:T(8,128)(2,1)S(1)}, bf16[8,4,32,384]{3,2,1,0:T(8,128)(2,1)}, u32[]{:S(2)}) copy-start(bf16[8,4,32,384]{3,2,1,0:T(8,128)(2,1)} %get-tuple-element.73) | copy-start | bytes 2359300
Sparse Core Ops, SparseCore 0:
  10.9 56.7 all-gather.1
  179.1 133.9 all-reduce.2
where the time goes:
time: 323 us; the launch traced here: 321 us
  waiting for transfers between devices  181 us (56%)
  matrix products  85.2 us (26%)
  local copies, waits for them, and re-layouts  28.3 us (9%)
  between operations  14.1 us (4%)
  other arithmetic  11.9 us (4%)
    unnamed x3, waiting for transfers between devices  128 us
    all_gather x1, waiting for transfers between devices, per_device(): gathered = lax.all_gather(bias_pair, ('dap', 'sub'), axis=1, tiled=True)  53 us
    sub x8, matrix products, row_grads(): attn_probs = jax.nn.softmax(scores, axis=-1)  20.7 us
    dot_general x8, matrix products, row_grads(): jnp.einsum('hdj,hdk->hjk', grad_att, value_row, preferred_element_type=jn...  18.9 us
    dot_general x8, matrix products, row_grads(): jnp.einsum('hjk,hdk->hdj', scores_low, key_row, preferred_element_type=jn...  14.6 us
    dot_general x8, matrix products, row_grads(): jnp.einsum('hjk,hdj->hdk', scores_low, query_row, preferred_element_type=...  11.3 us
    dot_general x8, matrix products, row_grads(): jnp.einsum('hjk,hdk->hdj', probs_low, value_row, preferred_element_type=j...  10.8 us
    while x5, local copies, waits for them, and re-layouts, per_device(): lax.scan(row_step, jnp.zeros(full_bias.shape, jnp.float32), stacked)  9.61 us
  transfers between devices with their start and end apart: 2, of which 2 were waited for; matrix products, arithmetic and copies ran while one was open for 4% of the time, Pallas kernels for 0%

commit v1 on v0

v1 whole, which is shorter than its diff:
```python
import functools

import jax
import jax.numpy as jnp
from jax import lax
from jax.experimental import pallas as pl
from jax.experimental.pallas import tpu as pltpu
from jax.sharding import PartitionSpec as P

F32 = jnp.float32
BF16 = jnp.bfloat16
MESH = pl.DeviceIdType.MESH
LANES = 128
PAD = 16


def dot(a, b, ca, cb):
    return lax.dot_general(a, b, (((ca,), (cb,)), ((), ())), preferred_element_type=F32)


def kernel(
    n_dap,
    q_ref,
    k_ref,
    v_ref,
    g_ref,
    go_ref,
    bias_ref,
    mask_ref,
    chain_col,
    chain_row,
    cb_ref,
    dq_ref,
    dk_ref,
    dv_ref,
    dg_ref,
    db_ref,
    qs,
    ks,
    vs,
    gas,
    gfs,
    oq,
    ok,
    ov,
    og,
    bias_t,
    acc,
    place,
    fixed,
    same,
    gath,
    snd,
    ra,
    sb,
    rb,
    g_send,
    g_recv,
    gf_send,
    gf_recv,
    a_send,
    a_recv,
    b_send,
    b_recv,
):
    heads, dh, rows, n = q_ref.shape
    own = db_ref.shape[1]
    scale = dh ** (-0.5)
    me = lax.axis_index("dap")
    core = lax.axis_index("sub")
    other = 1 - core

    def peer_of(t):
        return lax.rem(me + t, n_dap)

    barrier = pltpu.get_barrier_semaphore()

    def greet(t, carry):
        pl.semaphore_signal(barrier, inc=1, device_id={"dap": peer_of(t)}, device_id_type=MESH)
        return carry

    lax.fori_loop(1, n_dap, greet, 0)
    pl.semaphore_signal(barrier, inc=1, device_id={"sub": other}, device_id_type=MESH)

    def gather_copy(h, t):
        return pltpu.make_async_remote_copy(
            src_ref=bias_ref.at[h],
            dst_ref=gath.at[h, core, me],
            send_sem=g_send.at[h, t],
            recv_sem=g_recv.at[h, t],
            device_id={"dap": peer_of(t)},
            device_id_type=MESH,
        )

    def forward_copy(h):
        return pltpu.make_async_remote_copy(
            src_ref=gath.at[h, core],
            dst_ref=gath.at[h, core],
            send_sem=gf_send.at[h],
            recv_sem=gf_recv.at[h],
            device_id={"sub": other},
            device_id_type=MESH,
        )

    def core_copy(h):
        return pltpu.make_async_remote_copy(
            src_ref=snd.at[h, other],
            dst_ref=ra.at[h],
            send_sem=a_send.at[h],
            recv_sem=a_recv.at[h],
            device_id={"sub": other},
            device_id_type=MESH,
        )

    def owner_copy(h, t):
        return pltpu.make_async_remote_copy(
            src_ref=sb.at[h, peer_of(t)],
            dst_ref=rb.at[h, me],
            send_sem=b_send.at[h, t],
            recv_sem=b_recv.at[h, t],
            device_id={"dap": peer_of(t)},
            device_id_type=MESH,
        )

    def each_peer(h, make, what):
        def step(t, carry):
            what(make(h, t))
            return carry

        lax.fori_loop(1, n_dap, step, 0)

    pl.semaphore_wait(barrier, n_dap)
    for h in range(heads):
        each_peer(h, gather_copy, lambda c: c.start())
    for h in range(heads):
        gath[h, core, me] = bias_ref[h]

    def forward(h):
        each_peer(h, gather_copy, lambda c: c.wait_recv())
        forward_copy(h).start()

    def reduce_owner(h):
        core_copy(h).wait_recv()
        sb[h] = (snd[h, core].astype(F32) + ra[h].astype(F32)).astype(BF16)
        rb[h, me] = sb[h, me]
        each_peer(h, owner_copy, lambda c: c.start())

    total = 2 * n_dap * PAD
    r = lax.broadcasted_iota(jnp.int32, (total, n), 0)
    j = lax.broadcasted_iota(jnp.int32, (total, n), 1)
    half = jnp.where(r >= n_dap * PAD, 1, 0)
    slot = (r - half * (n_dap * PAD)) // PAD
    inner = r % PAD
    hit = (inner < own) & ((slot * 2 + half) * own + inner == j)
    place[...] = jnp.where(hit, 1.0, 0.0).astype(BF16)

    same[...] = jnp.where(chain_col[...] == chain_row[...], 1.0, 0.0)
    fixed[...] = jnp.where(mask_ref[...] > 0, 0.0, -1000000000.0).astype(F32)

    columns = n // LANES

    def flat(x):
        return x.astype(F32).reshape(dh * rows, n)

    def put(ref, x):
        for c in range(columns):
            ref[c] = x[:, c * LANES : (c + 1) * LANES]

    def take_row(ref, i):
        at = pl.ds(i, dh, stride=rows)
        return jnp.concatenate([ref[c, at, :] for c in range(columns)], axis=1)

    def put_row(ref, i, x):
        at = pl.ds(i, dh, stride=rows)
        for c in range(columns):
            ref[c, at, :] = x[:, c * LANES : (c + 1) * LANES]

    def prepare(h):
        put(qs, flat(q_ref[h]))
        put(ks, flat(k_ref[h]))
        put(vs, flat(v_ref[h]))
        gate = 1.0 / (1.0 + jnp.exp(-flat(g_ref[h])))
        cot = flat(go_ref[h])
        att = cot * gate
        put(gas, att)
        put(gfs, att * (1.0 - gate))

    def row(i):
        q = take_row(qs, i).astype(BF16)
        k = take_row(ks, i).astype(BF16)
        v = take_row(vs, i).astype(BF16)
        ga = take_row(gas, i).astype(BF16)
        s = dot(k, q, 0, 0) * scale + bias_t[...]
        e = jnp.exp(s - jnp.max(s, axis=0, keepdims=True))
        p = e * (1.0 / jnp.sum(e, axis=0, keepdims=True))
        low = p.astype(BF16)
        attended = dot(v, low, 1, 0)
        put_row(og, i, take_row(gfs, i) * attended)
        delta = jnp.sum(ga.astype(F32) * attended, axis=0, keepdims=True)
        put_row(ov, i, dot(ga, low, 1, 1))
        ds = p * (dot(v, ga, 0, 0) - delta)
        acc[...] += ds
        dlow = ds.astype(BF16)
        put_row(oq, i, dot(k, dlow, 1, 0) * scale)
        put_row(ok, i, dot(q, dlow, 1, 1) * scale)

    def some_rows(lo, hi):
        def step(i, carry):
            row(i)
            return carry

        lax.fori_loop(lo, hi, step, 0)

    early = rows // 2
    for h in range(heads):
        prepare(h)
        acc[...] = jnp.zeros_like(acc)
        if h == 0:
            forward(0)
        forward_copy(h).wait_recv()
        moved = dot(gath[h].reshape(total, n), place[...], 0, 0)
        bias_t[...] = moved + cb_ref[h] * same[...] + fixed[...]
        some_rows(0, early)
        if h + 1 < heads:
            forward(h + 1)
        if h > 0:
            reduce_owner(h - 1)
        some_rows(early, rows)
        out = dot(place[...], acc[...].astype(BF16), 1, 1)
        snd[h] = out.astype(BF16).reshape(2, n_dap, PAD, n)
        core_copy(h).start()

        for ref, held in ((dq_ref, oq), (dk_ref, ok), (dv_ref, ov), (dg_ref, og)):
            for c in range(columns):
                part = held[c].reshape(dh, rows, LANES).astype(BF16)
                ref[h, :, :, c * LANES : (c + 1) * LANES] = part
    reduce_owner(heads - 1)
    for h in range(heads):
        each_peer(h, owner_copy, lambda c: c.wait_recv())
        db_ref[h] = jnp.sum(rb[h].astype(F32), axis=0)[:own]
    for h in range(heads):
        each_peer(h, gather_copy, lambda c: c.wait_send())
        forward_copy(h).wait_send()
        core_copy(h).wait_send()
        each_peer(h, owner_copy, lambda c: c.wait_send())


def per_device(
    n_dap,
    query_act,
    key_act,
    value_act,
    gate_act,
    grad_out,
    bias_pair,
    residue_mask,
    chain_index,
    chain_bias,
):
    heads, dh, rows, n = query_act.shape
    own = bias_pair.shape[1]
    padded = jnp.pad(bias_pair, ((0, 0), (0, PAD - own), (0, 0)))
    vmem = pl.BlockSpec(memory_space=pltpu.VMEM)
    smem = pl.BlockSpec(memory_space=pltpu.SMEM)
    dma = pltpu.SemaphoreType.DMA
    act = jax.ShapeDtypeStruct(query_act.shape, BF16)
    flat = pltpu.VMEM((n // LANES, dh * rows, LANES), F32)
    return pl.pallas_call(
        functools.partial(kernel, n_dap),
        out_shape=(act, act, act, act, jax.ShapeDtypeStruct((heads, own, n), F32)),
        in_specs=[vmem] * 9 + [smem],
        out_specs=(vmem,) * 5,
        scratch_shapes=[flat] * 9
        + [
            pltpu.VMEM((n, n), F32),
            pltpu.VMEM((n, n), F32),
            pltpu.VMEM((2 * n_dap * PAD, n), BF16),
            pltpu.VMEM((n, 1), F32),
            pltpu.VMEM((n, n), F32),
            pltpu.VMEM((heads, 2, n_dap, PAD, n), BF16),
            pltpu.VMEM((heads, 2, n_dap, PAD, n), BF16),
            pltpu.VMEM((heads, n_dap, PAD, n), BF16),
            pltpu.VMEM((heads, n_dap, PAD, n), BF16),
            pltpu.VMEM((heads, n_dap, PAD, n), BF16),
            dma((heads, n_dap)),
            dma((heads, n_dap)),
            dma((heads,)),
            dma((heads,)),
            dma((heads,)),
            dma((heads,)),
            dma((heads, n_dap)),
            dma((heads, n_dap)),
        ],
        compiler_params=pltpu.CompilerParams(
            collective_id=0, has_side_effects=True, vmem_limit_bytes=56 * 2**20
        ),
        name="triangle_grads",
    )(
        query_act,
        key_act,
        value_act,
        gate_act,
        grad_out,
        padded,
        residue_mask[:, None],
        chain_index[:, None],
        chain_index[None, :],
        chain_bias,
    )


def solution(mesh):
    slab = P("ch", None, ("grp", "dap", "sub"), None)
    pair = P("ch", ("grp", "dap", "sub"), None)
    return jax.shard_map(
        functools.partial(per_device, mesh.shape["dap"]),
        mesh=mesh,
        in_specs=(slab,) * 5 + (pair, P("grp"), P("grp"), P("ch")),
        out_specs=(slab,) * 4 + (pair,),
        check_vma=False,
    )
```

time: 323 us -> 79.1 us (0.24)
  waiting for transfers between devices: 181 us -> 0 us
  matrix products: 85.2 us -> 0 us
  Pallas kernels: 0 us -> 66.3 us
  local copies, waits for them, and re-layouts: 28.3 us -> 11.7 us
  between operations: 14.1 us -> 0.65 us
  other arithmetic: 11.9 us -> 0 us
    unnamed x3 -> x0, waiting for transfers between devices: 128 us -> none
    pallas_call x0 -> x1, Pallas kernels: none -> 66.3 us  [per_device(): pl.pallas_call(functools.partial(kernel, n_dap), out_shape=(act, act, act...]
    dot_general x40 -> x0, matrix products: 64.5 us -> none  [the longest x8 18.9 us: row_grads(): jnp.einsum('hdj,hdk->hjk', grad_att, value_row, preferred_element_type=jn...]
    all_gather x1 -> x0, waiting for transfers between devices: 53 us -> none  [per_device(): gathered = lax.all_gather(bias_pair, ('dap', 'sub'), axis=1, tiled=True)]
    sub x8 -> x0, matrix products: 20.7 us -> none  [row_grads(): attn_probs = jax.nn.softmax(scores, axis=-1)]
    while x69 -> x0, local copies, waits for them, and re-layouts: 18.8 us -> none  [the longest x5 9.61 us: per_device(): lax.scan(row_step, jnp.zeros(full_bias.shape, jnp.float32), stacked)]
    dynamic_update_slice x8 -> x0, other arithmetic: 5.77 us -> none  [per_device(): lax.scan(row_step, jnp.zeros(full_bias.shape, jnp.float32), stacked)]
    convert_element_type x9 -> x0, other arithmetic: 3.39 us -> none  [the longest x1 1.71 us: pair_bias(): (chain_index[:, None] == chain_index[None, :]).astype(jnp.float32)]
  transfers between devices with their start and end apart: 2 -> 0, of which waited for: 2 -> 0; matrix products, arithmetic and copies ran while one was open for 4% -> 0% of each run, Pallas kernels for 0% -> 0%
where the time goes in v1:
time: 79.1 us; the launch traced here: 78.7 us
  Pallas kernels  66.3 us (84%)
  local copies, waits for them, and re-layouts  11.7 us (15%)
    pallas_call x1, Pallas kernels, per_device(): pl.pallas_call(functools.partial(kernel, n_dap), out_shape=(act, act, act...  66.3 us
    unnamed x15, local copies, waits for them, and re-layouts  6.7 us

profile of v1, /device:TPU:0, one launch (start us, length us, event | category | flops | bytes accessed | tf_op | source)
XLA Modules:
  0.0 78.7 jit_solution(2200218881907016885)
XLA Ops:
  0.6 1.2 %broadcast_in_dim.11.chain_row = s32[1,384]{1,0:T(1,128)} reshape(s32[384]{0:T(512)} %param.16) | data formatting | bytes 3072 | tf_op jit(solution)/shard_map/broadcast_in_dim | solution.py:307
  1.9 0.8 copy.16
  2.7 0.0 copy-start.4
  2.7 0.6 pad.4.bias_ref
  3.3 0.0 copy-done.4
  3.3 0.0 copy-start.3
  3.3 0.8 %broadcast_in_dim.12.mask_ref = s32[384,1]{1,0:T(8,128)} reshape(s32[384]{0:T(512)S(1)} %copy-done.4) | data formatting | bytes 3072 | tf_op jit(solution)/shard_map/broadcast_in_dim | solution.py:305
  4.1 0.0 copy-done.3
  4.1 0.8 %broadcast_in_dim.13.chain_col = s32[384,1]{1,0:T(8,128)} reshape(s32[384]{0:T(512)S(1)} %copy-done.3) | data formatting | bytes 3072 | tf_op jit(solution)/shard_map/broadcast_in_dim | solution.py:306
  4.9 66.3 %triangle_grads.1 = (bf16[4,32,8,384]{3,2,1,0:T(8,128)(2,1)}, bf16[4,32,8,384]{3,2,1,0:T(8,128)(2,1)}, bf16[4,32,8,384]{3,2,1,0:T(8,128)(2,1)}, bf16[4,32,8,384]{3,2,1,0:T(8,128)(2,1)}, f32[4,12,384]{2,1,0:T(8,128)}) custom-call(bf16[4,32,8,384]{3,2,1,0:T(8,128)(2,1)} %q_ref.1, bf16[4,32,8,384]{3,2,1,0:T(8,128)(2,1)} %k_ref.1, ...), custom_call_target="tpu_custom_call" | custom-call | tf_op jit(solution)/shard_map/triangle_grads/pallas_call | solution.py:268
  71.2 1.6 %copy.19 = f32[4,12,384]{2,0,1:T(4,128)} copy(f32[4,12,384]{2,1,0:T(8,128)} %get-tuple-element.14) | data formatting | bytes 147456 | tf_op jit(solution)/shard_map/triangle_grads/pallas_call | solution.py:268
  72.8 0.0 copy-start.2
  72.8 2.2 %copy.24 = bf16[4,32,8,384]{3,2,1,0:T(8,128)(2,1)} copy(bf16[4,32,8,384]{3,2,1,0:T(8,128)(2,1)} %get-tuple-element.20) | data formatting | bytes 1572864
  74.9 0.0 copy-done.2
  74.9 0.0 copy-start.1
  74.9 0.9 %copy.25 = bf16[4,32,8,384]{3,2,1,0:T(8,128)(2,1)} copy(bf16[4,32,8,384]{3,2,1,0:T(8,128)(2,1)S(1)} %copy-done.2) | data formatting | bytes 1572864
  75.8 0.5 copy-done.1
  76.4 0.0 copy-start
  76.4 0.9 %copy.26 = bf16[4,32,8,384]{3,2,1,0:T(8,128)(2,1)} copy(bf16[4,32,8,384]{3,2,1,0:T(8,128)(2,1)S(1)} %copy-done.1) | data formatting | bytes 1572864
  77.2 0.5 copy-done
  77.8 0.9 %copy.27 = bf16[4,32,8,384]{3,2,1,0:T(8,128)(2,1)} copy(bf16[4,32,8,384]{3,2,1,0:T(8,128)(2,1)S(1)} %copy-done) | data formatting | bytes 1572864
Async XLA Ops:
  2.7 0.7 copy-start.4
  3.3 0.8 %copy-start.3 = (s32[384]{0:T(512)S(1)}, s32[384]{0:T(512)}, u32[]{:S(2)}) copy-start(s32[384]{0:T(512)} %param.16) | copy-start | bytes 4612
  72.8 2.2 %copy-start.2 = (bf16[4,32,8,384]{3,2,1,0:T(8,128)(2,1)S(1)}, bf16[4,32,8,384]{3,2,1,0:T(8,128)(2,1)}, u32[]{:S(2)}) copy-start(bf16[4,32,8,384]{3,2,1,0:T(8,128)(2,1)} %get-tuple-element.21) | copy-start | bytes 2359300
  74.9 1.4 %copy-start.1 = (bf16[4,32,8,384]{3,2,1,0:T(8,128)(2,1)S(1)}, bf16[4,32,8,384]{3,2,1,0:T(8,128)(2,1)}, u32[]{:S(2)}) copy-start(bf16[4,32,8,384]{3,2,1,0:T(8,128)(2,1)} %get-tuple-element.22) | copy-start | bytes 2359300
  76.4 1.4 %copy-start = (bf16[4,32,8,384]{3,2,1,0:T(8,128)(2,1)S(1)}, bf16[4,32,8,384]{3,2,1,0:T(8,128)(2,1)}, u32[]{:S(2)}) copy-start(bf16[4,32,8,384]{3,2,1,0:T(8,128)(2,1)} %get-tuple-element.23) | copy-start | bytes 2359300

commit v2 on v1

v2 whole, which is shorter than its diff:
```python
import functools

import jax
import jax.numpy as jnp
from jax import lax
from jax.experimental import pallas as pl
from jax.experimental.pallas import tpu as pltpu
from jax.sharding import PartitionSpec as P

F32 = jnp.float32
BF16 = jnp.bfloat16
MESH = pl.DeviceIdType.MESH
LANES = 128
INNER = 4
PAD = 16


def dot(a, b, ca, cb):
    return lax.dot_general(a, b, (((ca,), (cb,)), ((), ())), preferred_element_type=F32)


def kernel(
    n_dap,
    q_hbm,
    k_hbm,
    v_hbm,
    g_hbm,
    go_hbm,
    rows_ref,
    mask_ref,
    chain_ref,
    cb_ref,
    dq_hbm,
    dk_hbm,
    dv_hbm,
    dg_hbm,
    db_ref,
    q_ref,
    k_ref,
    v_ref,
    g_ref,
    go_ref,
    dq_ref,
    dk_ref,
    dv_ref,
    dg_ref,
    bias_ref,
    qs,
    ks,
    vs,
    gas,
    gfs,
    oq,
    ok,
    ov,
    og,
    bias_t,
    acc,
    place,
    fixed,
    same,
    gath,
    snd,
    ra,
    sb,
    rb,
    sc,
    rc,
    in_sem,
    out_sem,
    g_send,
    g_recv,
    gi_send,
    gi_recv,
    gf_send,
    gf_recv,
    a_send,
    a_recv,
    b_send,
    b_recv,
    c_send,
    c_recv,
):
    heads, dh, rows, n = q_ref.shape
    own = db_ref.shape[0]
    scale = dh ** (-0.5)
    outer = n_dap // INNER
    me = lax.axis_index("dap")
    core = lax.axis_index("sub")
    other = 1 - core
    my_out = me // INNER
    my_in = lax.rem(me, INNER)

    moved_in = [
        pltpu.make_async_copy(src, dst, in_sem.at[x])
        for x, (src, dst) in enumerate(
            ((q_hbm, q_ref), (k_hbm, k_ref), (v_hbm, v_ref), (g_hbm, g_ref), (go_hbm, go_ref))
        )
    ]
    for copy in moved_in:
        copy.start()

    def out_of(t):
        return lax.rem(my_out + t, outer)

    def in_of(t):
        return lax.rem(my_in + t, INNER)

    def on_line(t):
        return {"dap": out_of(t) * INNER + my_in}

    def on_plane(t):
        return {"dap": my_out * INNER + in_of(t)}

    barrier = pltpu.get_barrier_semaphore()

    def greet(where):
        pl.semaphore_signal(barrier, inc=1, device_id=where, device_id_type=MESH)

    for t in range(1, outer):
        greet(on_line(t))
    for t in range(1, INNER):
        greet(on_plane(t))
    greet({"sub": other})

    def remote(src, dst, send, recv, where):
        return pltpu.make_async_remote_copy(
            src_ref=src,
            dst_ref=dst,
            send_sem=send,
            recv_sem=recv,
            device_id=where,
            device_id_type=MESH,
        )

    def line_copy(h, t):
        dst = gath.at[h, core, my_in, my_out]
        return remote(bias_ref.at[h], dst, g_send.at[h, t], g_recv.at[h, t], on_line(t))

    def plane_copy(h, t):
        held = gath.at[h, core, my_in]
        return remote(held, held, gi_send.at[h, t], gi_recv.at[h, t], on_plane(t))

    def forward_copy(h):
        held = gath.at[h, core]
        return remote(held, held, gf_send.at[h], gf_recv.at[h], {"sub": other})

    def core_copy(h):
        return remote(snd.at[h, other], ra.at[h], a_send.at[h], a_recv.at[h], {"sub": other})

    def plane_sum_copy(h, t):
        src, dst = sb.at[h, in_of(t)], rb.at[h, my_in]
        return remote(src, dst, b_send.at[h, t], b_recv.at[h, t], on_plane(t))

    def line_sum_copy(h, t):
        src, dst = sc.at[h, out_of(t)], rc.at[h, my_out]
        return remote(src, dst, c_send.at[h, t], c_recv.at[h, t], on_line(t))

    def lines(h, make, what):
        for t in range(1, outer):
            what(make(h, t))

    def planes(h, make, what):
        for t in range(1, INNER):
            what(make(h, t))

    def start(c):
        c.start()

    def arrive(c):
        c.wait_recv()

    def left(c):
        c.wait_send()

    mine = rows_ref[...].astype(F32)
    for h in range(heads):
        block = jnp.concatenate([mine[:, h, :], jnp.zeros((PAD - own, n), F32)], axis=0)
        bias_ref[h] = block.astype(BF16)

    pl.semaphore_wait(barrier, outer + INNER - 1)
    for h in range(heads):
        lines(h, line_copy, start)
    for h in range(heads):
        gath[h, core, my_in, my_out] = bias_ref[h]

    def to_plane(h):
        lines(h, line_copy, arrive)
        planes(h, plane_copy, start)

    def to_core(h):
        planes(h, plane_copy, arrive)
        forward_copy(h).start()

    def sum_cores(h):
        core_copy(h).wait_recv()
        sb[h] = (snd[h, core].astype(F32) + ra[h].astype(F32)).astype(BF16)
        rb[h, my_in] = sb[h, my_in]
        planes(h, plane_sum_copy, start)

    def sum_plane(h):
        planes(h, plane_sum_copy, arrive)
        sc[h] = jnp.sum(rb[h].astype(F32), axis=0).astype(BF16)
        rc[h, my_out] = sc[h, my_out]
        lines(h, line_sum_copy, start)

    def sum_line(h):
        lines(h, line_sum_copy, arrive)
        db_ref[:, h, :] = jnp.sum(rc[h].astype(F32), axis=0)[:own]

    total = 2 * n_dap * PAD
    r = lax.broadcasted_iota(jnp.int32, (total, n), 0)
    j = lax.broadcasted_iota(jnp.int32, (total, n), 1)
    half = jnp.where(r >= n_dap * PAD, 1, 0)
    held = (r - half * (n_dap * PAD)) // PAD
    inner = r % PAD
    slot = (held % outer) * INNER + held // outer
    hit = (inner < own) & ((slot * 2 + half) * own + inner == j)
    place[...] = jnp.where(hit, 1.0, 0.0).astype(BF16)

    def wide(x):
        return jnp.broadcast_to(x.reshape(1, n), (8, n))

    chain = wide(chain_ref[...].astype(F32))
    same[...] = jnp.where(chain.T[:, :1] == chain[:1], 1.0, 0.0)
    blocked = wide(jnp.where(mask_ref[...] > 0, 0.0, -1000000000.0).astype(F32))
    fixed[...] = blocked.T[:, :1]

    columns = n // LANES

    def flat(x):
        return x.astype(F32).reshape(dh * rows, n)

    def put(ref, x):
        for c in range(columns):
            ref[c] = x[:, c * LANES : (c + 1) * LANES]

    def take_row(ref, i):
        at = pl.ds(i, dh, stride=rows)
        return jnp.concatenate([ref[c, at, :] for c in range(columns)], axis=1)

    def put_row(ref, i, x):
        at = pl.ds(i, dh, stride=rows)
        for c in range(columns):
            ref[c, at, :] = x[:, c * LANES : (c + 1) * LANES]

    def prepare(h):
        put(qs, flat(q_ref[h]))
        put(ks, flat(k_ref[h]))
        put(vs, flat(v_ref[h]))
        gate = 1.0 / (1.0 + jnp.exp(-flat(g_ref[h])))
        cot = flat(go_ref[h])
        att = cot * gate
        put(gas, att)
        put(gfs, att * (1.0 - gate))

    def row(i):
        q = take_row(qs, i).astype(BF16)
        k = take_row(ks, i).astype(BF16)
        v = take_row(vs, i).astype(BF16)
        ga = take_row(gas, i).astype(BF16)
        s = dot(k, q, 0, 0) * scale + bias_t[...]
        e = jnp.exp(s - jnp.max(s, axis=0, keepdims=True))
        p = e * (1.0 / jnp.sum(e, axis=0, keepdims=True))
        low = p.astype(BF16)
        attended = dot(v, low, 1, 0)
        put_row(og, i, take_row(gfs, i) * attended)
        delta = jnp.sum(ga.astype(F32) * attended, axis=0, keepdims=True)
        put_row(ov, i, dot(ga, low, 1, 1))
        ds = p * (dot(v, ga, 0, 0) - delta)
        acc[...] += ds
        dlow = ds.astype(BF16)
        put_row(oq, i, dot(k, dlow, 1, 0) * scale)
        put_row(ok, i, dot(q, dlow, 1, 1) * scale)

    def some_rows(lo, hi):
        def step(i, carry):
            row(i)
            return carry

        lax.fori_loop(lo, hi, step, 0)

    outs = [(dq_ref, oq, dq_hbm), (dk_ref, ok, dk_hbm), (dv_ref, ov, dv_hbm), (dg_ref, og, dg_hbm)]

    def out_copy(h, x):
        return pltpu.make_async_copy(outs[x][0].at[h], outs[x][2].at[h], out_sem.at[h, x])

    to_plane(0)
    for copy in moved_in:
        copy.wait()
    for h in range(heads):
        prepare(h)
        acc[...] = jnp.zeros_like(acc)
        if h == 0:
            to_core(0)
        forward_copy(h).wait_recv()
        moved = dot(gath[h].reshape(total, n), place[...], 0, 0)
        bias_t[...] = moved + cb_ref[h] * same[...] + fixed[...]
        some_rows(0, rows // 4)
        if h + 1 < heads:
            to_plane(h + 1)
        if h > 0:
            sum_cores(h - 1)
        some_rows(rows // 4, rows * 5 // 8)
        if h + 1 < heads:
            to_core(h + 1)
        if h > 0:
            sum_plane(h - 1)
        some_rows(rows * 5 // 8, rows)
        if h > 0:
            sum_line(h - 1)
        out = dot(place[...], acc[...].astype(BF16), 1, 1)
        snd[h] = out.astype(BF16).reshape(2, INNER, outer, PAD, n)
        core_copy(h).start()
        for x, (ref, held, _) in enumerate(outs):
            for c in range(columns):
                part = held[c].reshape(dh, rows, LANES).astype(BF16)
                ref[h, :, :, c * LANES : (c + 1) * LANES] = part
            out_copy(h, x).start()
    sum_cores(heads - 1)
    sum_plane(heads - 1)
    sum_line(heads - 1)
    for h in range(heads):
        for x in range(4):
            out_copy(h, x).wait()
        lines(h, line_copy, left)
        planes(h, plane_copy, left)
        forward_copy(h).wait_send()
        core_copy(h).wait_send()
        planes(h, plane_sum_copy, left)
        lines(h, line_sum_copy, left)


def per_device(
    n_dap,
    query_act,
    key_act,
    value_act,
    gate_act,
    grad_out,
    bias_pair,
    residue_mask,
    chain_index,
    chain_bias,
):
    heads, dh, rows, n = query_act.shape
    own = bias_pair.shape[1]
    outer = n_dap // INNER
    vmem = pl.BlockSpec(memory_space=pltpu.VMEM)
    smem = pl.BlockSpec(memory_space=pltpu.SMEM)
    hbm = pl.BlockSpec(memory_space=pl.ANY)
    dma = pltpu.SemaphoreType.DMA
    act = jax.ShapeDtypeStruct(query_act.shape, BF16)
    flat = pltpu.VMEM((n // LANES, dh * rows, LANES), F32)
    *grads, grad_bias = pl.pallas_call(
        functools.partial(kernel, n_dap),
        out_shape=(act, act, act, act, jax.ShapeDtypeStruct((own, heads, n), F32)),
        in_specs=[hbm] * 5 + [vmem] * 3 + [smem],
        out_specs=(hbm,) * 4 + (vmem,),
        scratch_shapes=[pltpu.VMEM(query_act.shape, BF16)] * 9
        + [pltpu.VMEM((heads, PAD, n), BF16)]
        + [flat] * 9
        + [
            pltpu.VMEM((n, n), F32),
            pltpu.VMEM((n, n), F32),
            pltpu.VMEM((2 * n_dap * PAD, n), BF16),
            pltpu.VMEM((n, 1), F32),
            pltpu.VMEM((n, n), F32),
            pltpu.VMEM((heads, 2, INNER, outer, PAD, n), BF16),
            pltpu.VMEM((heads, 2, INNER, outer, PAD, n), BF16),
            pltpu.VMEM((heads, INNER, outer, PAD, n), BF16),
            pltpu.VMEM((heads, INNER, outer, PAD, n), BF16),
            pltpu.VMEM((heads, INNER, outer, PAD, n), BF16),
            pltpu.VMEM((heads, outer, PAD, n), BF16),
            pltpu.VMEM((heads, outer, PAD, n), BF16),
            dma((5,)),
            dma((heads, 4)),
            dma((heads, outer)),
            dma((heads, outer)),
            dma((heads, INNER)),
            dma((heads, INNER)),
            dma((heads,)),
            dma((heads,)),
            dma((heads,)),
            dma((heads,)),
            dma((heads, INNER)),
            dma((heads, INNER)),
            dma((heads, outer)),
            dma((heads, outer)),
        ],
        compiler_params=pltpu.CompilerParams(
            collective_id=0, has_side_effects=True, vmem_limit_bytes=56 * 2**20
        ),
        name="triangle_grads",
    )(
        query_act,
        key_act,
        value_act,
        gate_act,
        grad_out,
        jnp.swapaxes(bias_pair, 0, 1),
        residue_mask,
        chain_index,
        chain_bias,
    )
    return (*grads, jnp.swapaxes(grad_bias, 0, 1))


def solution(mesh):
    slab = P("ch", None, ("grp", "dap", "sub"), None)
    pair = P("ch", ("grp", "dap", "sub"), None)
    return jax.shard_map(
        functools.partial(per_device, mesh.shape["dap"]),
        mesh=mesh,
        in_specs=(slab,) * 5 + (pair, P("grp"), P("grp"), P("ch")),
        out_specs=(slab,) * 4 + (pair,),
        check_vma=False,
    )
```

time: 79.1 us -> 78.9 us (level)
  local copies, waits for them, and re-layouts: 11.7 us -> 6.56 us
  Pallas kernels: 66.3 us -> 71.3 us
    pallas_call x1, Pallas kernels: 66.3 us -> 71.3 us  [per_device(): pl.pallas_call(functools.partial(kernel, n_dap), out_shape=(act, act, act...]
    broadcast_in_dim x3 -> x0, local copies, waits for them, and re-layouts: 2.83 us -> none  [the longest x1 1.25 us: per_device(): chain_index[None, :]]
    pallas_call x1 -> x0, local copies, waits for them, and re-layouts: 1.56 us -> none  [per_device(): pl.pallas_call(functools.partial(kernel, n_dap), out_shape=(act, act, act...]
    unnamed x15 -> x13, local copies, waits for them, and re-layouts: 6.7 us -> 6.56 us
where the time goes in v2:
time: 78.9 us; the launch traced here: 78.5 us
  Pallas kernels  71.3 us (90%)
  local copies, waits for them, and re-layouts  6.56 us (8%)
    pallas_call x1, Pallas kernels, per_device(): pl.pallas_call(functools.partial(kernel, n_dap), out_shape=(act, act, act...  71.3 us
    unnamed x13, local copies, waits for them, and re-layouts  6.56 us

profile of v2, /device:TPU:0, one launch (start us, length us, event | category | flops | bytes accessed | tf_op | source)
XLA Modules:
  0.0 78.5 jit_solution(18426976952140648461)
XLA Ops:
  0.6 71.3 %triangle_grads.1 = (bf16[4,32,8,384]{3,2,1,0:T(8,128)(2,1)}, bf16[4,32,8,384]{3,2,1,0:T(8,128)(2,1)}, bf16[4,32,8,384]{3,2,1,0:T(8,128)(2,1)}, bf16[4,32,8,384]{3,2,1,0:T(8,128)(2,1)}, f32[12,4,384]{2,1,0:T(4,128)}) custom-call(bf16[4,32,8,384]{3,2,1,0:T(8,128)(2,1)} %q_hbm.1, bf16[4,32,8,384]{3,2,1,0:T(8,128)(2,1)} %k_hbm.1, ...), custom_call_target="tpu_custom_call" | custom-call | tf_op jit(solution)/shard_map/triangle_grads/pallas_call | solution.py:355
  71.9 0.0 copy-start.2
  71.9 2.2 %copy.19 = bf16[4,32,8,384]{3,2,1,0:T(8,128)(2,1)} copy(bf16[4,32,8,384]{3,2,1,0:T(8,128)(2,1)} %get-tuple-element.20) | data formatting | bytes 1572864
  74.1 0.0 copy-done.2
  74.1 0.0 copy-start.1
  74.1 0.9 %copy.20 = bf16[4,32,8,384]{3,2,1,0:T(8,128)(2,1)} copy(bf16[4,32,8,384]{3,2,1,0:T(8,128)(2,1)S(1)} %copy-done.2) | data formatting | bytes 1572864
  75.0 0.5 copy-done.1
  75.5 0.0 copy-start
  75.5 0.9 %copy.21 = bf16[4,32,8,384]{3,2,1,0:T(8,128)(2,1)} copy(bf16[4,32,8,384]{3,2,1,0:T(8,128)(2,1)S(1)} %copy-done.1) | data formatting | bytes 1572864
  76.4 0.5 copy-done
  76.9 0.0 copy-start.3
  76.9 0.9 %copy.22 = bf16[4,32,8,384]{3,2,1,0:T(8,128)(2,1)} copy(bf16[4,32,8,384]{3,2,1,0:T(8,128)(2,1)S(1)} %copy-done) | data formatting | bytes 1572864
  77.8 0.1 copy-done.3
  77.9 0.6 copy.23
Async XLA Ops:
  71.9 2.2 %copy-start.2 = (bf16[4,32,8,384]{3,2,1,0:T(8,128)(2,1)S(1)}, bf16[4,32,8,384]{3,2,1,0:T(8,128)(2,1)}, u32[]{:S(2)}) copy-start(bf16[4,32,8,384]{3,2,1,0:T(8,128)(2,1)} %get-tuple-element.21) | copy-start | bytes 2359300
  74.1 1.4 %copy-start.1 = (bf16[4,32,8,384]{3,2,1,0:T(8,128)(2,1)S(1)}, bf16[4,32,8,384]{3,2,1,0:T(8,128)(2,1)}, u32[]{:S(2)}) copy-start(bf16[4,32,8,384]{3,2,1,0:T(8,128)(2,1)} %get-tuple-element.22) | copy-start | bytes 2359300
  75.5 1.4 %copy-start = (bf16[4,32,8,384]{3,2,1,0:T(8,128)(2,1)S(1)}, bf16[4,32,8,384]{3,2,1,0:T(8,128)(2,1)}, u32[]{:S(2)}) copy-start(bf16[4,32,8,384]{3,2,1,0:T(8,128)(2,1)} %get-tuple-element.23) | copy-start | bytes 2359300
  76.9 0.9 %copy-start.3 = (f32[12,4,384]{2,1,0:T(4,128)S(1)}, f32[12,4,384]{2,1,0:T(4,128)}, u32[]{:S(2)}) copy-start(f32[12,4,384]{2,1,0:T(4,128)} %get-tuple-element.14) | copy-start | bytes 221188

commit v3 on v2

--- a/solution.py
+++ b/solution.py
@@ -11,7 +11,7 @@
 BF16 = jnp.bfloat16
 MESH = pl.DeviceIdType.MESH
 LANES = 128
-INNER = 4
+PARTS = 2
 PAD = 16
 
 
@@ -64,32 +64,23 @@
     ra,
     sb,
     rb,
-    sc,
-    rc,
     in_sem,
     out_sem,
     g_send,
     g_recv,
-    gi_send,
-    gi_recv,
     gf_send,
     gf_recv,
     a_send,
     a_recv,
     b_send,
     b_recv,
-    c_send,
-    c_recv,
 ):
     heads, dh, rows, n = q_ref.shape
     own = db_ref.shape[0]
     scale = dh ** (-0.5)
-    outer = n_dap // INNER
     me = lax.axis_index("dap")
     core = lax.axis_index("sub")
     other = 1 - core
-    my_out = me // INNER
-    my_in = lax.rem(me, INNER)
 
     moved_in = [
         pltpu.make_async_copy(src, dst, in_sem.at[x])
@@ -100,28 +91,17 @@
     for copy in moved_in:
         copy.start()
 
-    def out_of(t):
-        return lax.rem(my_out + t, outer)
-
-    def in_of(t):
-        return lax.rem(my_in + t, INNER)
-
-    def on_line(t):
-        return {"dap": out_of(t) * INNER + my_in}
-
-    def on_plane(t):
-        return {"dap": my_out * INNER + in_of(t)}
+    def peer(t):
+        return lax.rem(me + t, n_dap)
 
     barrier = pltpu.get_barrier_semaphore()
 
-    def greet(where):
-        pl.semaphore_signal(barrier, inc=1, device_id=where, device_id_type=MESH)
-
-    for t in range(1, outer):
-        greet(on_line(t))
-    for t in range(1, INNER):
-        greet(on_plane(t))
-    greet({"sub": other})
+    def greet(t, carry):
+        pl.semaphore_signal(barrier, inc=1, device_id={"dap": peer(t)}, device_id_type=MESH)
+        return carry
+
+    lax.fori_loop(1, n_dap, greet, 0)
+    pl.semaphore_signal(barrier, inc=1, device_id={"sub": other}, device_id_type=MESH)
 
     def remote(src, dst, send, recv, where):
         return pltpu.make_async_remote_copy(
@@ -133,13 +113,9 @@
             device_id_type=MESH,
         )
 
-    def line_copy(h, t):
-        dst = gath.at[h, core, my_in, my_out]
-        return remote(bias_ref.at[h], dst, g_send.at[h, t], g_recv.at[h, t], on_line(t))
-
-    def plane_copy(h, t):
-        held = gath.at[h, core, my_in]
-        return remote(held, held, gi_send.at[h, t], gi_recv.at[h, t], on_plane(t))
+    def gather_copy(h, t):
+        dst = gath.at[h, core, me]
+        return remote(bias_ref.at[h], dst, g_send.at[h, t], g_recv.at[h, t], {"dap": peer(t)})
 
     def forward_copy(h):
         held = gath.at[h, core]
@@ -148,21 +124,16 @@
     def core_copy(h):
         return remote(snd.at[h, other], ra.at[h], a_send.at[h], a_recv.at[h], {"sub": other})
 
-    def plane_sum_copy(h, t):
-        src, dst = sb.at[h, in_of(t)], rb.at[h, my_in]
-        return remote(src, dst, b_send.at[h, t], b_recv.at[h, t], on_plane(t))
-
-    def line_sum_copy(h, t):
-        src, dst = sc.at[h, out_of(t)], rc.at[h, my_out]
-        return remote(src, dst, c_send.at[h, t], c_recv.at[h, t], on_line(t))
-
-    def lines(h, make, what):
-        for t in range(1, outer):
+    def owner_copy(h, t):
+        src, dst = sb.at[h, peer(t)], rb.at[h, me]
+        return remote(src, dst, b_send.at[h, t], b_recv.at[h, t], {"dap": peer(t)})
+
+    def peers(h, make, what):
+        def step(t, carry):
             what(make(h, t))
-
-    def planes(h, make, what):
-        for t in range(1, INNER):
-            what(make(h, t))
+            return carry
+
+        lax.fori_loop(1, n_dap, step, 0)
 
     def start(c):
         c.start()
@@ -178,43 +149,33 @@
         block = jnp.concatenate([mine[:, h, :], jnp.zeros((PAD - own, n), F32)], axis=0)
         bias_ref[h] = block.astype(BF16)
 
-    pl.semaphore_wait(barrier, outer + INNER - 1)
-    for h in range(heads):
-        lines(h, line_copy, start)
-    for h in range(heads):
-        gath[h, core, my_in, my_out] = bias_ref[h]
-
-    def to_plane(h):
-        lines(h, line_copy, arrive)
-        planes(h, plane_copy, start)
-
-    def to_core(h):
-        planes(h, plane_copy, arrive)
+    pl.semaphore_wait(barrier, n_dap)
+    peers(0, gather_copy, start)
+    for h in range(heads):
+        gath[h, core, me] = bias_ref[h]
+
+    def forward(h):
+        peers(h, gather_copy, arrive)
         forward_copy(h).start()
+        if h + 1 < heads:
+            peers(h + 1, gather_copy, start)
 
     def sum_cores(h):
         core_copy(h).wait_recv()
         sb[h] = (snd[h, core].astype(F32) + ra[h].astype(F32)).astype(BF16)
-        rb[h, my_in] = sb[h, my_in]
-        planes(h, plane_sum_copy, start)
-
-    def sum_plane(h):
-        planes(h, plane_sum_copy, arrive)
-        sc[h] = jnp.sum(rb[h].astype(F32), axis=0).astype(BF16)
-        rc[h, my_out] = sc[h, my_out]
-        lines(h, line_sum_copy, start)
-
-    def sum_line(h):
-        lines(h, line_sum_copy, arrive)
-        db_ref[:, h, :] = jnp.sum(rc[h].astype(F32), axis=0)[:own]
+        rb[h, me] = sb[h, me]
+        peers(h, owner_copy, start)
+
+    def sum_owner(h):
+        peers(h, owner_copy, arrive)
+        db_ref[:, h, :] = jnp.sum(rb[h].astype(F32), axis=0)[:own]
 
     total = 2 * n_dap * PAD
     r = lax.broadcasted_iota(jnp.int32, (total, n), 0)
     j = lax.broadcasted_iota(jnp.int32, (total, n), 1)
     half = jnp.where(r >= n_dap * PAD, 1, 0)
-    held = (r - half * (n_dap * PAD)) // PAD
+    slot = (r - half * (n_dap * PAD)) // PAD
     inner = r % PAD
-    slot = (held % outer) * INNER + held // outer
     hit = (inner < own) & ((slot * 2 + half) * own + inner == j)
     place[...] = jnp.where(hit, 1.0, 0.0).astype(BF16)
 
@@ -275,42 +236,36 @@
 
     def some_rows(lo, hi):
         def step(i, carry):
-            row(i)
+            row(2 * i)
+            row(2 * i + 1)
             return carry
 
-        lax.fori_loop(lo, hi, step, 0)
+        lax.fori_loop(lo // 2, hi // 2, step, 0)
 
     outs = [(dq_ref, oq, dq_hbm), (dk_ref, ok, dk_hbm), (dv_ref, ov, dv_hbm), (dg_ref, og, dg_hbm)]
 
     def out_copy(h, x):
         return pltpu.make_async_copy(outs[x][0].at[h], outs[x][2].at[h], out_sem.at[h, x])
 
-    to_plane(0)
     for copy in moved_in:
         copy.wait()
+    early = rows // 4 * 2
     for h in range(heads):
         prepare(h)
         acc[...] = jnp.zeros_like(acc)
         if h == 0:
-            to_core(0)
+            forward(0)
         forward_copy(h).wait_recv()
         moved = dot(gath[h].reshape(total, n), place[...], 0, 0)
         bias_t[...] = moved + cb_ref[h] * same[...] + fixed[...]
-        some_rows(0, rows // 4)
+        some_rows(0, early)
         if h + 1 < heads:
-            to_plane(h + 1)
+            forward(h + 1)
         if h > 0:
             sum_cores(h - 1)
-        some_rows(rows // 4, rows * 5 // 8)
-        if h + 1 < heads:
-            to_core(h + 1)
-        if h > 0:
-            sum_plane(h - 1)
-        some_rows(rows * 5 // 8, rows)
-        if h > 0:
-            sum_line(h - 1)
+        some_rows(early, rows)
         out = dot(place[...], acc[...].astype(BF16), 1, 1)
-        snd[h] = out.astype(BF16).reshape(2, INNER, outer, PAD, n)
+        snd[h] = out.astype(BF16).reshape(2, n_dap, PAD, n)
         core_copy(h).start()
         for x, (ref, held, _) in enumerate(outs):
             for c in range(columns):
@@ -318,17 +273,40 @@
                 ref[h, :, :, c * LANES : (c + 1) * LANES] = part
             out_copy(h, x).start()
     sum_cores(heads - 1)
-    sum_plane(heads - 1)
-    sum_line(heads - 1)
+    for h in range(heads):
+        sum_owner(h)
     for h in range(heads):
         for x in range(4):
             out_copy(h, x).wait()
-        lines(h, line_copy, left)
-        planes(h, plane_copy, left)
+        peers(h, gather_copy, left)
         forward_copy(h).wait_send()
         core_copy(h).wait_send()
-        planes(h, plane_sum_copy, left)
-        lines(h, line_sum_copy, left)
+        peers(h, owner_copy, left)
+
+
+def place_results(*refs):
+    sources, results, held = refs[:5], refs[5:10], refs[10:15]
+    in_sem, out_sem = refs[15:]
+    pieces = []
+    for x in range(5):
+        parts = PARTS if x < 4 else 1
+        for part in range(parts):
+            if x < 4:
+                depth = held[x].shape[1] // PARTS
+                at = (slice(None), pl.ds(part * depth, depth))
+            else:
+                at = (slice(None),)
+            mine = held[x].at[at]
+            fetch = pltpu.make_async_copy(sources[x].at[at], mine, in_sem.at[x, part])
+            store = pltpu.make_async_copy(mine, results[x].at[at], out_sem.at[x, part])
+            pieces.append((fetch, store))
+    for fetch, _ in pieces:
+        fetch.start()
+    for fetch, store in pieces:
+        fetch.wait()
+        store.start()
+    for _, store in pieces:
+        store.wait()
 
 
 def per_device(
@@ -345,7 +323,6 @@
 ):
     heads, dh, rows, n = query_act.shape
     own = bias_pair.shape[1]
-    outer = n_dap // INNER
     vmem = pl.BlockSpec(memory_space=pltpu.VMEM)
     smem = pl.BlockSpec(memory_space=pltpu.SMEM)
     hbm = pl.BlockSpec(memory_space=pl.ANY)
@@ -366,27 +343,21 @@
             pltpu.VMEM((2 * n_dap * PAD, n), BF16),
             pltpu.VMEM((n, 1), F32),
             pltpu.VMEM((n, n), F32),
-            pltpu.VMEM((heads, 2, INNER, outer, PAD, n), BF16),
-            pltpu.VMEM((heads, 2, INNER, outer, PAD, n), BF16),
-            pltpu.VMEM((heads, INNER, outer, PAD, n), BF16),
-            pltpu.VMEM((heads, INNER, outer, PAD, n), BF16),
-            pltpu.VMEM((heads, INNER, outer, PAD, n), BF16),
-            pltpu.VMEM((heads, outer, PAD, n), BF16),
-            pltpu.VMEM((heads, outer, PAD, n), BF16),
+            pltpu.VMEM((heads, 2, n_dap, PAD, n), BF16),
+            pltpu.VMEM((heads, 2, n_dap, PAD, n), BF16),
+            pltpu.VMEM((heads, n_dap, PAD, n), BF16),
+            pltpu.VMEM((heads, n_dap, PAD, n), BF16),
+            pltpu.VMEM((heads, n_dap, PAD, n), BF16),
             dma((5,)),
             dma((heads, 4)),
-            dma((heads, outer)),
-            dma((heads, outer)),
-            dma((heads, INNER)),
-            dma((heads, INNER)),
+            dma((heads, n_dap)),
+            dma((heads, n_dap)),
             dma((heads,)),
             dma((heads,)),
             dma((heads,)),
             dma((heads,)),
-            dma((heads, INNER)),
-            dma((heads, INNER)),
-            dma((heads, outer)),
-            dma((heads, outer)),
+            dma((heads, n_dap)),
+            dma((heads, n_dap)),
         ],
         compiler_params=pltpu.CompilerParams(
             collective_id=0, has_side_effects=True, vmem_limit_bytes=56 * 2**20
@@ -403,6 +374,16 @@
         chain_index,
         chain_bias,
     )
+    *grads, grad_bias = pl.pallas_call(
+        place_results,
+        out_shape=(act, act, act, act, jax.ShapeDtypeStruct((own, heads, n), F32)),
+        in_specs=[hbm] * 5,
+        out_specs=(hbm,) * 5,
+        scratch_shapes=[pltpu.VMEM(query_act.shape, BF16)] * 4
+        + [pltpu.VMEM((own, heads, n), F32), dma((5, PARTS)), dma((5, PARTS))],
+        compiler_params=pltpu.CompilerParams(vmem_limit_bytes=60 * 2**20),
+        name="place_results",
+    )(*grads, grad_bias)
     return (*grads, jnp.swapaxes(grad_bias, 0, 1))
 
 

time: 78.9 us -> 63.7 us (0.81)
  Pallas kernels: 71.3 us -> 62.7 us
  local copies, waits for them, and re-layouts: 6.56 us -> 0 us
    pallas_call x1, Pallas kernels: 71.3 us -> 59.8 us  [per_device(): pl.pallas_call(functools.partial(kernel, n_dap), out_shape=(act, act, act...]
    unnamed x13 -> x0, local copies, waits for them, and re-layouts: 6.56 us -> none
    pallas_call x0 -> x1, Pallas kernels: none -> 2.84 us  [per_device(): pl.pallas_call(place_results, out_shape=(act, act, act, act, jax.ShapeDty...]
where the time goes in v3:
time: 63.7 us; the launch traced here: 63.5 us
  Pallas kernels  62.7 us (98%)
  between operations  0.8 us (1%)
    pallas_call x1, Pallas kernels, per_device(): pl.pallas_call(functools.partial(kernel, n_dap), out_shape=(act, act, act...  59.8 us
    pallas_call x1, Pallas kernels, per_device(): pl.pallas_call(place_results, out_shape=(act, act, act, act, jax.ShapeDty...  2.84 us

profile of v3, /device:TPU:0, one launch (start us, length us, event | category | flops | bytes accessed | tf_op | source)
XLA Modules:
  0.0 63.5 jit_solution(18092922117933830221)
XLA Ops:
  0.6 59.8 %triangle_grads.1 = (bf16[4,32,8,384]{3,2,1,0:T(8,128)(2,1)}, bf16[4,32,8,384]{3,2,1,0:T(8,128)(2,1)}, bf16[4,32,8,384]{3,2,1,0:T(8,128)(2,1)}, bf16[4,32,8,384]{3,2,1,0:T(8,128)(2,1)}, f32[12,4,384]{2,1,0:T(4,128)}) custom-call(bf16[4,32,8,384]{3,2,1,0:T(8,128)(2,1)} %q_hbm.1, bf16[4,32,8,384]{3,2,1,0:T(8,128)(2,1)} %k_hbm.1, ...), custom_call_target="tpu_custom_call" | custom-call | tf_op jit(solution)/shard_map/triangle_grads/pallas_call | solution.py:332
  60.5 2.8 %place_results.1 = (bf16[4,32,8,384]{3,2,1,0:T(8,128)(2,1)}, bf16[4,32,8,384]{3,2,1,0:T(8,128)(2,1)}, bf16[4,32,8,384]{3,2,1,0:T(8,128)(2,1)}, bf16[4,32,8,384]{3,2,1,0:T(8,128)(2,1)}, f32[12,4,384]{2,1,0:T(4,128)}) custom-call(bf16[4,32,8,384]{3,2,1,0:T(8,128)(2,1)} %get-tuple-element.15.refs_0_, bf16[4,32,8,384]{3,2,1,0:T(8,128)(2,1)} %get-tuple-element.16.refs_1_, ...), custom_call_target="tpu_custom_call" | custom-call | tf_op jit(solution)/shard_map/place_results/pallas_call | solution.py:377

commit v4 on v3

--- a/solution.py
+++ b/solution.py
@@ -247,14 +247,14 @@
     def out_copy(h, x):
         return pltpu.make_async_copy(outs[x][0].at[h], outs[x][2].at[h], out_sem.at[h, x])
 
-    for copy in moved_in:
-        copy.wait()
     early = rows // 4 * 2
     for h in range(heads):
+        if h == 0:
+            forward(0)
+            for copy in moved_in:
+                copy.wait()
         prepare(h)
         acc[...] = jnp.zeros_like(acc)
-        if h == 0:
-            forward(0)
         forward_copy(h).wait_recv()
         moved = dot(gath[h].reshape(total, n), place[...], 0, 0)
         bias_t[...] = moved + cb_ref[h] * same[...] + fixed[...]

time: 63.7 us -> 63.7 us (level)
  no operation moved by 1% of the time
where the time goes in v4:
time: 63.7 us; the launch traced here: 63.5 us
  Pallas kernels  62.7 us (98%)
  between operations  0.8 us (1%)
    pallas_call x1, Pallas kernels, per_device(): pl.pallas_call(functools.partial(kernel, n_dap), out_shape=(act, act, act...  59.8 us
    pallas_call x1, Pallas kernels, per_device(): pl.pallas_call(place_results, out_shape=(act, act, act, act, jax.ShapeDty...  2.84 us

profile of v4, /device:TPU:0, one launch (start us, length us, event | category | flops | bytes accessed | tf_op | source)
XLA Modules:
  0.0 63.5 jit_solution(12428128813874708147)
XLA Ops:
  0.6 59.8 %triangle_grads.1 = (bf16[4,32,8,384]{3,2,1,0:T(8,128)(2,1)}, bf16[4,32,8,384]{3,2,1,0:T(8,128)(2,1)}, bf16[4,32,8,384]{3,2,1,0:T(8,128)(2,1)}, bf16[4,32,8,384]{3,2,1,0:T(8,128)(2,1)}, f32[12,4,384]{2,1,0:T(4,128)}) custom-call(bf16[4,32,8,384]{3,2,1,0:T(8,128)(2,1)} %q_hbm.1, bf16[4,32,8,384]{3,2,1,0:T(8,128)(2,1)} %k_hbm.1, ...), custom_call_target="tpu_custom_call" | custom-call | tf_op jit(solution)/shard_map/triangle_grads/pallas_call | solution.py:332
  60.5 2.8 %place_results.1 = (bf16[4,32,8,384]{3,2,1,0:T(8,128)(2,1)}, bf16[4,32,8,384]{3,2,1,0:T(8,128)(2,1)}, bf16[4,32,8,384]{3,2,1,0:T(8,128)(2,1)}, bf16[4,32,8,384]{3,2,1,0:T(8,128)(2,1)}, f32[12,4,384]{2,1,0:T(4,128)}) custom-call(bf16[4,32,8,384]{3,2,1,0:T(8,128)(2,1)} %get-tuple-element.15.refs_0_, bf16[4,32,8,384]{3,2,1,0:T(8,128)(2,1)} %get-tuple-element.16.refs_1_, ...), custom_call_target="tpu_custom_call" | custom-call | tf_op jit(solution)/shard_map/place_results/pallas_call | solution.py:377
